TPU v7x, 128 devices: a whole 4x4x4 slice. The times are simulated.
128 devices in a mesh: sp: 16 (over z, y), hd: 8 (over x, core).
Axes of the slice: x: 4, y: 4, z: 4, core: 2. Of those that a mesh axis runs over, the one named last changes fastest.
Arguments:
- latent: bfloat16 [8, 64, 64, 320], P(None, 'sp', 'hd'), may hold values from -6 to 6
- condition: bfloat16 [8, 64, 64, 192], P(None, 'sp', 'hd'), may hold values from -6 to 6
- text_states: bfloat16 [8, 77, 768], replicated, may hold values from -6 to 6
- valid_rows: int32 [8], replicated, may hold values from 16 to 64, as said below
- text_lengths: int32 [8], replicated, may hold values from 8 to 77, as said below
- w_in: bfloat16 [192, 320], replicated, may hold values from -0.4375 to 0.4375
- b_in: float32 [320], replicated, may hold values from -3 to 3
- w_conv: bfloat16 [3, 3, 320, 320], replicated, may hold values from -0.109375 to 0.109375
- b_conv: float32 [320], replicated, may hold values from -3 to 3
- w_out: bfloat16 [320, 320], replicated, may hold values from -0.3125 to 0.3125
- b_out: float32 [320], replicated, may hold values from -3 to 3
- w_query: bfloat16 [320, 320], replicated, may hold values from -0.3125 to 0.3125
- w_key: bfloat16 [320, 320], replicated, may hold values from -0.3125 to 0.3125
- w_value: bfloat16 [320, 320], replicated, may hold values from -0.3125 to 0.3125
- w_attn_out: bfloat16 [320, 320], replicated, may hold values from -6 to 6
- b_attn_out: float32 [320], replicated, may hold values from -3 to 3
- w_cross_query: bfloat16 [320, 320], replicated, may hold values from -0.3125 to 0.3125
- w_cross_key: bfloat16 [768, 320], replicated, may hold values from -0.21875 to 0.21875
- w_cross_value: bfloat16 [768, 320], replicated, may hold values from -0.21875 to 0.21875
- w_cross_out: bfloat16 [320, 320], replicated, may hold values from -2 to 2
- b_cross_out: float32 [320], replicated, may hold values from -3 to 3
- w_ff_in: bfloat16 [320, 2560], replicated, may hold values from -0.3125 to 0.3125
- b_ff_in: float32 [2560], replicated, may hold values from -3 to 3
- w_ff_out: bfloat16 [1280, 320], replicated, may hold values from -0.15625 to 0.15625
- b_ff_out: float32 [320], replicated, may hold values from -3 to 3
- cotangent: bfloat16 [8, 64, 64, 320], P(None, 'sp', 'hd'), may hold values from -6 to 6
Outputs:
- mixed_out: bfloat16 [8, 64, 64, 320], P(None, 'sp', 'hd')
- latent_grad: float32 [8, 64, 64, 320], P(None, 'sp', 'hd')
- grad_w_in: float32 [192, 320], replicated
- grad_b_in: float32 [320], replicated
- grad_w_conv: float32 [3, 3, 320, 320], replicated
- grad_b_conv: float32 [320], replicated
- grad_w_out: float32 [320, 320], replicated
- grad_b_out: float32 [320], replicated
Inputs may be any that keep to these rules, and one draw needn't show every extreme that they name: `valid_rows`: some item has all 64 rows valid. The first text_lengths[item] tokens are valid; some item has all 77.
All inputs are finite; a program needn't handle non-finite values.
Results may differ from a plain program's by a relative error of at most 0.012.
Values may be sent and summed in bfloat16 or wider, within the bound.
No kernel may reach another device: no remote copies, remote signals or barrier semaphores. Data moves between devices by JAX's collectives and lax.ppermute only.
A program may use at most 128 MiB of HBM per device.

v0:
```python
import jax
import jax.numpy as jnp
from jax import lax
from jax.sharding import PartitionSpec as P

HEADS = 8


epsilon = 1e-05
masked_score = -1e30


def padded(cells, sides, width):
    for axis, dim in sides:
        count = lax.axis_size(axis)
        ends = count - 1
        head = lax.slice_in_dim(cells, 0, width, axis=dim)
        tail = lax.slice_in_dim(cells, cells.shape[dim] - width, cells.shape[dim], axis=dim)
        cells = jnp.concatenate(
            [
                lax.ppermute(tail, axis, [(i, (i + 1) % count) for i in range(ends)]),
                cells,
                lax.ppermute(head, axis, [((i + 1) % count, i) for i in range(ends)]),
            ],
            axis=dim,
        )
    return cells


def project(source, weight):
    return jnp.einsum("...c,cd->...d", source, weight, preferred_element_type=jnp.float32)


def project_back(source, weight):
    return jnp.einsum("...d,cd->...c", source, weight, preferred_element_type=jnp.float32)


def outer_sum(source, grads):
    flat_source = source.reshape(-1, source.shape[-1])
    flat_grads = grads.reshape(-1, grads.shape[-1])
    return jnp.einsum("nc,nd->cd", flat_source, flat_grads, preferred_element_type=jnp.float32)


def normalize(values):
    center = values - jnp.mean(values, -1, keepdims=True)
    variance = jnp.mean(center * center, -1, keepdims=True)
    return center * lax.rsqrt(variance + epsilon)


def paired(array):
    return array.reshape((array.shape[0] // 2, 2) + array.shape[1:])


def unpaired(array):
    return array.reshape((array.shape[0] * 2,) + array.shape[2:])


def scores_of(queries, keys_all, key_keep, scaling):
    raw = (
        jnp.einsum("bqhd,bkhd->bhqk", queries, keys_all, preferred_element_type=jnp.float32)
        * scaling
    )
    return jnp.where(key_keep[:, None, None, :], raw, masked_score)


def attend_back(queries, grads, keys_all, values_all, key_keep, logsum, weighted, scaling):
    probs = jnp.exp(scores_of(queries, keys_all, key_keep, scaling) - logsum)
    grad_probs = jnp.einsum(
        "bqhd,bkhd->bhqk", grads, values_all, preferred_element_type=jnp.float32
    )
    weighted = jnp.sum(probs * grad_probs, -1, keepdims=True)
    grad_scores = (probs * (grad_probs - weighted)).astype(jnp.bfloat16)
    return (probs, grad_scores, weighted)


def per_device(
    latent,
    condition,
    text_states,
    valid_rows,
    text_lengths,
    w_in,
    b_in,
    w_conv,
    b_conv,
    w_out,
    b_out,
    w_query,
    w_key,
    w_value,
    w_attn_out,
    b_attn_out,
    w_cross_query,
    w_cross_key,
    w_cross_value,
    w_cross_out,
    b_cross_out,
    w_ff_in,
    b_ff_in,
    w_ff_out,
    b_ff_out,
    cotangent,
):
    item_count, row_count, col_count, channels = latent.shape
    head_size = channels // HEADS
    heads_here = HEADS // lax.axis_size("hd")
    head_channels = heads_here * head_size
    scaling = head_size ** (-0.5)
    all_cols = col_count * lax.axis_size("hd")
    all_rows = row_count * lax.axis_size("sp")
    local_len = row_count * all_cols
    full_len = all_rows * all_cols
    text_count = text_states.shape[1]
    pre_start = project(condition, w_in) + b_in
    start = pre_start.astype(jnp.bfloat16)
    rimmed = padded(start, (("sp", 1), ("hd", 2)), 1)
    patches = jnp.concatenate(
        [
            rimmed[:, row_shift : row_shift + row_count, col_shift : col_shift + col_count]
            for row_shift in range(3)
            for col_shift in range(3)
        ],
        axis=-1,
    )
    inner = project(patches, w_conv.reshape(9 * channels, channels)) + b_conv
    smooth_float, silu_back = jax.vjp(jax.nn.silu, inner)
    smooth = smooth_float.astype(jnp.bfloat16)
    mixed = latent.astype(jnp.float32) + (
        start.astype(jnp.float32) + project(smooth, w_out) + b_out
    )
    normed, norm_back_one = jax.vjp(normalize, mixed)
    normed_low = normed.astype(jnp.bfloat16)
    triple = jnp.stack(
        [project(normed_low, weight).astype(jnp.bfloat16) for weight in (w_query, w_key, w_value)]
    )
    by_head = lax.all_to_all(triple, "hd", split_axis=4, concat_axis=3, tiled=True)
    own_pair = by_head[1:]
    gathered = lax.all_gather(own_pair, "sp", axis=2, tiled=True)
    queries = by_head[0].reshape(item_count, local_len, heads_here, head_size)
    keys_all = gathered[0].reshape(item_count, full_len, heads_here, head_size)
    values_all = gathered[1].reshape(item_count, full_len, heads_here, head_size)
    key_keep = (jnp.arange(full_len) // all_cols)[None, :] < valid_rows[:, None]

    def forward_pair(pair_block):
        pair_q, pair_k, pair_v, pair_keep = pair_block
        scores = scores_of(pair_q, pair_k, pair_keep, scaling)
        row_max = jnp.max(scores, -1, keepdims=True)
        shifted = jnp.exp(scores - row_max)
        row_total = jnp.sum(shifted, -1, keepdims=True)
        attended = jnp.einsum(
            "bhqk,bkhd->bqhd",
            (shifted / row_total).astype(jnp.bfloat16),
            pair_v,
            preferred_element_type=jnp.float32,
        )
        return (attended.astype(jnp.bfloat16), row_max + jnp.log(row_total))

    attended, logsum = lax.map(
        forward_pair, (paired(queries), paired(keys_all), paired(values_all), paired(key_keep))
    )
    attended = unpaired(attended)
    logsum = unpaired(logsum)
    back_heads = lax.all_to_all(
        attended.reshape(item_count, row_count, all_cols, head_channels),
        "hd",
        split_axis=2,
        concat_axis=3,
        tiled=True,
    )
    first = mixed + project(back_heads, w_attn_out) + b_attn_out
    normed_two, norm_back_two = jax.vjp(normalize, first)
    cross_q = (
        project(normed_two.astype(jnp.bfloat16), w_cross_query)
        .astype(jnp.bfloat16)
        .reshape(item_count, row_count * col_count, HEADS, head_size)
    )
    text_keys = (
        project(text_states, w_cross_key)
        .astype(jnp.bfloat16)
        .reshape(item_count, text_count, HEADS, head_size)
    )
    text_values = (
        project(text_states, w_cross_value)
        .astype(jnp.bfloat16)
        .reshape(item_count, text_count, HEADS, head_size)
    )
    text_keep = jnp.arange(text_count)[None, :] < text_lengths[:, None]
    cross_probs = jax.nn.softmax(scores_of(cross_q, text_keys, text_keep, scaling), axis=-1)
    cross_out = jnp.einsum(
        "bhqk,bkhd->bqhd",
        cross_probs.astype(jnp.bfloat16),
        text_values,
        preferred_element_type=jnp.float32,
    )
    cross_out = cross_out.astype(jnp.bfloat16).reshape(item_count, row_count, col_count, channels)
    second = first + project(cross_out, w_cross_out) + b_cross_out
    normed_three, norm_back_three = jax.vjp(normalize, second)
    gate_up = project(normed_three.astype(jnp.bfloat16), w_ff_in) + b_ff_in
    hidden_units = w_ff_out.shape[0]

    def geglu(joined):
        return joined[..., :hidden_units] * jax.nn.gelu(
            joined[..., hidden_units:], approximate=False
        )

    activated, geglu_back = jax.vjp(geglu, gate_up)
    result = second + project(activated.astype(jnp.bfloat16), w_ff_out) + b_ff_out
    grad_act = project_back(cotangent, w_ff_out)
    grad_gate_up = geglu_back(grad_act)[0].astype(jnp.bfloat16)
    grad_second = (
        cotangent.astype(jnp.float32) + norm_back_three(project_back(grad_gate_up, w_ff_in))[0]
    )
    grad_cross_out = project_back(grad_second.astype(jnp.bfloat16), w_cross_out).astype(
        jnp.bfloat16
    )
    grad_cross_out = grad_cross_out.reshape(item_count, row_count * col_count, HEADS, head_size)
    grad_cross_probs = jnp.einsum(
        "bqhd,bkhd->bhqk", grad_cross_out, text_values, preferred_element_type=jnp.float32
    )
    cross_weighted = jnp.sum(cross_probs * grad_cross_probs, -1, keepdims=True)
    grad_cross_scores = (cross_probs * (grad_cross_probs - cross_weighted)).astype(jnp.bfloat16)
    grad_cross_q = scaling * jnp.einsum(
        "bhqk,bkhd->bqhd", grad_cross_scores, text_keys, preferred_element_type=jnp.float32
    )
    grad_cross_q = grad_cross_q.astype(jnp.bfloat16).reshape(
        item_count, row_count, col_count, channels
    )
    grad_first = grad_second + norm_back_two(project_back(grad_cross_q, w_cross_query))[0]
    grad_self_out = project_back(grad_first.astype(jnp.bfloat16), w_attn_out).astype(jnp.bfloat16)
    grad_heads = lax.all_to_all(
        grad_self_out, "hd", split_axis=3, concat_axis=2, tiled=True
    ).reshape(item_count, local_len, heads_here, head_size)
    regathered = lax.all_gather(own_pair, "sp", axis=2, tiled=True)
    keys_back = regathered[0].reshape(item_count, full_len, heads_here, head_size)
    values_back = regathered[1].reshape(item_count, full_len, heads_here, head_size)

    def summed_pair(pair_block):
        pair_q, pair_g, pair_k, pair_v, pair_keep, pair_log = pair_block
        probs, grad_scores, weighted = attend_back(
            pair_q, pair_g, pair_k, pair_v, pair_keep, pair_log, None, scaling
        )
        query_part = scaling * jnp.einsum(
            "bhqk,bkhd->bqhd", grad_scores, pair_k, preferred_element_type=jnp.float32
        )
        key_part = scaling * jnp.einsum(
            "bhqk,bqhd->bkhd", grad_scores, pair_q, preferred_element_type=jnp.float32
        )
        value_part = jnp.einsum(
            "bhqk,bqhd->bkhd",
            probs.astype(jnp.bfloat16),
            pair_g,
            preferred_element_type=jnp.float32,
        )
        return (query_part.astype(jnp.bfloat16), key_part, value_part)

    mapped = lax.map(
        summed_pair,
        (
            paired(queries),
            paired(grad_heads),
            paired(keys_back),
            paired(values_back),
            paired(key_keep),
            paired(logsum),
        ),
    )
    query_grad = unpaired(mapped[0])
    partial_kv = jnp.stack([unpaired(mapped[1]), unpaired(mapped[2])]).reshape(
        2, item_count, all_rows, all_cols, head_channels
    )
    own_grads = lax.psum_scatter(
        partial_kv.astype(jnp.bfloat16), "sp", scatter_dimension=2, tiled=True
    )
    key_grad_own = own_grads[0]
    value_grad_own = own_grads[1]
    query_grad_rows = query_grad.reshape(item_count, row_count, all_cols, head_channels)
    triple_grad = jnp.stack([query_grad_rows, key_grad_own, value_grad_own])
    back_grads = lax.all_to_all(triple_grad, "hd", split_axis=3, concat_axis=4, tiled=True)
    grad_normed = (
        project_back(back_grads[0], w_query)
        + project_back(back_grads[1], w_key)
        + project_back(back_grads[2], w_value)
    )
    latent_grad = grad_first + norm_back_one(grad_normed)[0]
    grad_branch = latent_grad.astype(jnp.bfloat16)
    grad_w_out = outer_sum(smooth, grad_branch)
    grad_b_out = jnp.sum(latent_grad, axis=(0, 1, 2))
    grad_inner = silu_back(project_back(grad_branch, w_out))[0].astype(jnp.bfloat16)
    grad_b_conv = jnp.sum(grad_inner.astype(jnp.float32), axis=(0, 1, 2))
    grad_w_conv = outer_sum(patches, grad_inner).reshape(3, 3, channels, channels)
    grad_rim = padded(grad_inner, (("sp", 1), ("hd", 2)), 1)
    shifted_grads = jnp.concatenate(
        [
            grad_rim[
                :,
                2 - row_shift : 2 - row_shift + row_count,
                2 - col_shift : 2 - col_shift + col_count,
            ]
            for row_shift in range(3)
            for col_shift in range(3)
        ],
        axis=-1,
    )
    flipped = w_conv.transpose(0, 1, 3, 2).reshape(9 * channels, channels)
    grad_start = (latent_grad + project(shifted_grads, flipped)).astype(jnp.bfloat16)
    grad_w_in = outer_sum(condition, grad_start)
    grad_b_in = jnp.sum(grad_start.astype(jnp.float32), axis=(0, 1, 2))
    totals = lax.psum(
        (grad_w_in, grad_b_in, grad_w_conv, grad_b_conv, grad_w_out, grad_b_out), ("sp", "hd")
    )
    return (
        result.astype(jnp.bfloat16),
        latent_grad,
        totals[0],
        totals[1],
        totals[2],
        totals[3],
        totals[4],
        totals[5],
    )


def solution(mesh):
    in_specs = (
        P(None, "sp", "hd", None),
        P(None, "sp", "hd", None),
        P(),
        P(),
        P(),
        P(),
        P(),
        P(),
        P(),
        P(),
        P(),
        P(),
        P(),
        P(),
        P(),
        P(),
        P(),
        P(),
        P(),
        P(),
        P(),
        P(),
        P(),
        P(),
        P(),
        P(None, "sp", "hd", None),
    )
    out_specs = (P(None, "sp", "hd", None), P(None, "sp", "hd", None), P(), P(), P(), P(), P(), P())
    return jax.shard_map(
        per_device, mesh=mesh, in_specs=in_specs, out_specs=out_specs, check_vma=False
    )
```

profile of v0, /device:TPU:1, one launch (start us, length us, event | category | flops | bytes accessed | tf_op | source)
XLA Modules:
  0.0 808.5 jit_solution(17246958401670416131)
XLA Ops:
  34.5 8.2 %copy.109 = bf16[3,8,4,8,320]{3,2,1,0,4:T(4,128)(2,1)} copy(bf16[3,8,4,8,320]{4,3,2,1,0:T(8,128)(2,1)S(1)} %pad_maximum_fusion.3) | data formatting | bytes 983040 | tf_op jit(solution)/shard_map/stack | solution.py:133
  42.7 10.0 %reshape.341 = bf16[8,2,15360]{2,1,0:T(2,128)(2,1)S(1)} reshape(bf16[320,3,8,4,8]{4,3,2,1,0:T(4,128)(2,1)} %bitcast.332) | data formatting | bytes 983040
  52.7 14.9 %all_to_all.63 = bf16[8,2,15360]{2,1,0:T(2,128)(2,1)S(1)} all-to-all(bf16[8,2,15360]{2,1,0:T(2,128)(2,1)S(1)} %reshape.341), channel_id=1, replica_groups=mesh['sp'=16,'hd'=8] {'hd'}, dimensions={0} | all-to-all | bytes 983040 | tf_op jit(solution)/shard_map/all_to_all | solution.py:136
  67.7 10.1 %reshape.342 = bf16[320,3,8,4,8]{4,3,2,1,0:T(4,128)(2,1)} reshape(bf16[8,2,15360]{2,1,0:T(2,128)(2,1)S(1)} %all_to_all.63) | data formatting | bytes 983040
  77.8 10.9 %copy.110 = bf16[3,8,4,8,8,40]{5,3,4,2,1,0:T(8,128)(2,1)} copy(bf16[3,8,4,8,8,40]{3,2,1,0,5,4:T(4,128)(2,1)} %bitcast.333) | data formatting | bytes 983040 | tf_op jit(solution)/shard_map/all_to_all | solution.py:136
  98.8 107.3 %all-gather.2.cloned.1.call-done = bf16[2,8,64,64,40]{4,3,2,1,0:T(8,128)(2,1)} async-done(((bf16[2,8,4,64,40]{4,3,2,1,0:T(8,128)(2,1)}), bf16[2,8,64,64,40]{4,3,2,1,0:T(8,128)(2,1)}) %all-gather.2.cloned.1.call-update) | async-done | bytes 5242896 | tf_op jit(solution)/shard_map/all_gather | solution.py:138
  206.1 12.7 %fusion.130 = (bf16[1,8,64,64,40]{4,3,2,1,0:T(8,128)(2,1)}, bf16[1,8,64,64,40]{4,3,2,1,0:T(8,128)(2,1)}) fusion(bf16[2,8,64,64,40]{4,3,2,1,0:T(8,128)(2,1)} %all-gather.2.cloned.1.call-done), kind=kLoop, calls=%fused_computation.237 | loop fusion | bytes 10485760 | tf_op jit(solution)/shard_map/slice | solution.py:140
  218.9 8.1 %copy.111 = bf16[4,2,4096,1,40]{2,4,1,3,0:T(8,128)(2,1)} copy(bf16[4,2,4096,1,40]{4,2,1,0,3:T(8,128)(2,1)} %bitcast.331) | data formatting | bytes 5242880 | tf_op jit(solution)/shard_map/while | solution.py:158
  227.0 8.1 %copy.113 = bf16[4,2,4096,1,40]{2,4,1,3,0:T(8,128)(2,1)} copy(bf16[4,2,4096,1,40]{4,2,1,0,3:T(8,128)(2,1)} %bitcast.330) | data formatting | bytes 5242880 | tf_op jit(solution)/shard_map/while | solution.py:158
  235.2 34.2 %while.26 = (s32[]{:T(128)}, bf16[4,2,256,1,40]{2,4,1,3,0:T(8,128)(2,1)S(1)}, f32[4,2,1,256,1]{3,1,4,2,0:T(2,128)}, bf16[4,2,4096,1,40]{2,4,1,3,0:T(8,128)(2,1)}...) while((s32[]{:T(128)}, ...), condition=%wide.region_5.6_spmd, body=%wide.region_2.5_spmd.sunk | while | flops 360730112 | bytes 26634340 | solution.py:158
  324.6 7.0 reshape.345
  349.6 99.2 %while.27 = (s32[]{:T(128)}, bf16[4,2,256,1,40]{2,4,1,3,0:T(8,128)(2,1)S(1)}, bf16[4,2,4096,1,40]{2,4,1,3,0:T(8,128)(2,1)}, bf16[4,2,4096,1,40]{2,4,1,3,0:T(8,12...) while((s32[]{:T(128)}, ...), condition=%wide.region_19.20_spmd, body=%wide.region_17.19_spmd.sunk | while | flops 858103296 | bytes 155835664 | solution.py:256
  352.7 6.9 multiply_reduce_fusion.9
  359.6 7.9 multiply_convert_fusion.14
  384.4 7.9 multiply_convert_fusion.14
  409.2 7.9 multiply_convert_fusion.14
  433.9 7.9 multiply_convert_fusion.14
  448.8 8.4 %stack.28 = bf16[1,8,64,64,40]{3,2,4,1,0:T(8,128)(2,1)} reshape(bf16[4,2,4096,1,40]{2,4,1,3,0:T(8,128)(2,1)} %get-tuple-element.104) | data formatting | bytes 5242880 | tf_op jit(solution)/shard_map/stack | solution.py:268
  457.2 8.5 %stack.27 = bf16[1,8,64,64,40]{3,2,4,1,0:T(8,128)(2,1)} reshape(bf16[4,2,4096,1,40]{2,4,1,3,0:T(8,128)(2,1)} %get-tuple-element.103) | data formatting | bytes 5242880 | tf_op jit(solution)/shard_map/stack | solution.py:268
  465.7 10.4 %pad_maximum_fusion = bf16[2,8,64,64,40]{3,2,4,1,0:T(8,128)(2,1)} fusion(bf16[1,8,64,64,40]{3,2,4,1,0:T(8,128)(2,1)} %stack.28, bf16[1,8,64,64,40]{3,2,4,1,0:T(8,128)(2,1)} %stack.27), kind=kLoop, calls=%fused_computation.59 | loop fusion | flops 2621440 | bytes 10485760 | tf_op jit(solution)/shard_map/stack | solution.py:268
  476.2 14.6 %copy.131 = bf16[2,8,64,64,40]{3,4,1,0,2:T(8,128)(2,1)} copy(bf16[2,8,64,64,40]{3,2,4,1,0:T(8,128)(2,1)} %pad_maximum_fusion) | data formatting | bytes 10485760 | tf_op jit(solution)/shard_map/stack | solution.py:268
  491.0 87.3 %reduce-scatter.2.cloned.1.call-done = bf16[2,8,4,64,40]{3,4,1,0,2:T(8,128)(2,1)} async-done(((bf16[2,8,64,64,40]{3,4,1,0,2:T(8,128)(2,1)}), bf16[2,8,4,64,40]{3,4,1,0,2:T(8,128)(2,1)}) %reduce-scatter.2.cloned.1.call-update) | async-done | bytes 327696 | tf_op jit(solution)/shard_map/reduce_scatter | solution.py:271
  641.8 66.6 %all-reduce.2 = (f32[320]{0:T(512)}, f32[320]{0:T(512)}, f32[320]{0:T(512)}) all-reduce(f32[320]{0:T(512)S(1)} %get-tuple-element.256, f32[320]{0:T(512)S(1)} %get-tuple-element.258, f32[320]{0:T(512)S(1)} %get-tuple-element.196), channel_id=1, replica_groups=mesh['sp'=16,'hd'=8] {'sp','hd'}, use_global_device_ids=true, to_apply=%region_25.26 | all-reduce | flops 960 | bytes 7680 | tf_op jit(solution)/shard_map/psum | solution.py:308
  708.4 86.0 %all-reduce.6.cloned.1.call-done = (f32[192,320]{1,0:T(8,128)}, f32[3,3,320,320]{3,2,1,0:T(8,128)}, f32[320,320]{1,0:T(8,128)}) async-done(((f32[192,320]{1,0:T(8,128)}, f32[3,3,320,320]{3,2,1,0:T(8,128)}, f32[320,320]{1,0:T(8,128)}), (f32[192,320]{1,0:T(8,128)}, f32[3,3,320,320]{3,2,1,0:T(8,128)}, f32[320,320]{1,0:T(8,128)})) %all-reduce.6.cloned.1.call-update) | async-done | bytes 4341776 | tf_op jit(solution)/shard_map/psum | solution.py:308
  (346 shorter events, 275.0 us)
Async XLA Ops:
  7.2 295.6 %copy-start = (bf16[320,2560]{1,0:T(8,128)(2,1)S(1)}, bf16[320,2560]{1,0:T(8,128)(2,1)}, u32[]{:S(2)}) copy-start(bf16[320,2560]{1,0:T(8,128)(2,1)} %param.51) | copy-start | bytes 4915204
  7.2 199.0 %all-gather.2.cloned.1.call-start = ((), (), s32[]{:S(2)}) async-start(), calls=%async_computation.5 | async-start | bytes 17825792 | tf_op jit(solution)/shard_map/all_gather | solution.py:138
  8.6 6.0 collective-permute-start.1
  9.9 5.8 collective-permute-start
  15.8 7.7 collective-permute-start.3
  19.6 4.5 collective-permute-start.2
  32.3 252.2 %copy-start.4 = (f32[8,4,8,320]{3,2,1,0:T(8,128)}, f32[8,4,8,320]{3,2,1,0:T(8,128)S(1)}, u32[]{:S(2)}) copy-start(f32[8,4,8,320]{3,2,1,0:T(8,128)S(1)} %get-tuple-element.240) | copy-start | bytes 983044
  269.4 7.4 copy-start.62
  271.6 10.7 %all-to-all-start.1 = ((bf16[8,2,5120]{2,1,0:T(2,128)(2,1)}), bf16[8,2,5120]{2,1,0:T(2,128)(2,1)S(1)}, u32[]{:S(2)}, u32[]{:S(2)}) async-start(bf16[8,2,5120]{2,1,0:T(2,128)(2,1)} %reshape.343), calls=%async_computation.1 | async-start | bytes 327680 | tf_op jit(solution)/shard_map/all_to_all | solution.py:163
  302.5 7.3 copy-start.6
  331.6 9.8 %all-to-all-start.2 = ((bf16[8,2,5120]{2,1,0:T(2,128)(2,1)}), bf16[8,2,5120]{2,1,0:T(2,128)(2,1)S(1)}, u32[]{:S(2)}, u32[]{:S(2)}) async-start(bf16[8,2,5120]{2,1,0:T(2,128)(2,1)} %reshape.345), calls=%async_computation.2 | async-start | bytes 327680 | tf_op jit(solution)/shard_map/all_to_all | solution.py:230
  335.8 242.5 %reduce-scatter.2.cloned.1.call-start = ((), (), s32[]{:S(2)}) async-start(), calls=%async_computation.6 | async-start | bytes 11141120 | tf_op jit(solution)/shard_map/reduce_scatter | solution.py:271
  352.0 7.6 copy-start.3
  376.8 7.5 copy-start.3
  401.6 7.6 copy-start.3
  426.4 7.5 copy-start.3
  585.4 14.8 %all-to-all-start.3 = ((bf16[8,2,15360]{2,1,0:T(2,128)(2,1)}), bf16[8,2,15360]{2,1,0:T(2,128)(2,1)}, u32[]{:S(2)}, u32[]{:S(2)}) async-start(bf16[8,2,15360]{2,1,0:T(2,128)(2,1)} %reshape.347), calls=%async_computation.4 | async-start | bytes 983040 | tf_op jit(solution)/shard_map/all_to_all | solution.py:278
  591.0 203.4 %all-reduce.6.cloned.1.call-start = ((), (), s32[]{:S(2)}) async-start(), calls=%async_computation.7 | async-start | bytes 10420224 | tf_op jit(solution)/shard_map/psum | solution.py:308
  611.1 9.2 %copy-start.38 = (f32[8,4,8,320]{3,2,1,0:T(8,128)}, f32[8,4,8,320]{3,2,1,0:T(8,128)S(1)}, u32[]{:S(2)}) copy-start(f32[8,4,8,320]{3,2,1,0:T(8,128)S(1)} %get-tuple-element.433) | copy-start | bytes 983044
  611.4 5.8 copy-start.10
  611.8 9.5 %collective-permute-start.5 = (bf16[8,1,8,320]{3,2,1,0:T(8,128)(2,1)S(1)}, bf16[8,1,8,320]{3,2,1,0:T(8,128)(2,1)S(1)}, u32[]{:S(2)}, u32[]{:S(2)}) collective-permute-start(bf16[8,1,8,320]{3,2,1,0:T(8,128)(2,1)S(1)} %get-tuple-element.234), channel_id=1, source_target_pairs={{8,0},{16,8},{24,16},{32,24},{40,32},{48,40},{56,48},{64,56},{72,6... | collective-permute-start | bytes 122888 | tf_op jit(solution)/shard_map/ppermute | solution.py:23
  613.3 8.1 %collective-permute-start.4 = (bf16[8,1,8,320]{3,2,1,0:T(8,128)(2,1)S(1)}, bf16[8,1,8,320]{3,2,1,0:T(8,128)(2,1)S(1)}, u32[]{:S(2)}, u32[]{:S(2)}) collective-permute-start(bf16[8,1,8,320]{3,2,1,0:T(8,128)(2,1)S(1)} %get-tuple-element.233), channel_id=1, source_target_pairs={{0,8},{8,16},{16,24},{24,32},{32,40},{40,48},{48,56},{56,64},{64,7... | collective-permute-start | bytes 122888 | tf_op jit(solution)/shard_map/ppermute | solution.py:21
  621.5 6.5 collective-permute-start.7
  625.0 5.7 collective-permute-start.6
  (67 other events, 135.2 us)
Sparse Core Ops, SparseCore 0:
  91.2 114.9 all-gather.1
  490.9 87.3 reduce-scatter.1
  637.4 157.0 all-reduce.5
where the time goes:
time: 817 us; the launch traced here: 808 us
  waiting for transfers between devices  299 us (37%)
  local copies, waits for them, and re-layouts  185 us (23%)
  matrix products  127 us (16%)
  blocking collectives  81.6 us (10%)
  other arithmetic  61.1 us (7%)
  starting transfers between devices  38.9 us (5%)
  between operations  15.2 us (2%)
    all_gather x1, waiting for transfers between devices, per_device(): gathered = lax.all_gather(own_pair, 'sp', axis=2, tiled=True)  107 us
    reduce_scatter x1, waiting for transfers between devices, per_device(): lax.psum_scatter(partial_kv.astype(jnp.bfloat16), 'sp', scatter_dimension...  87.3 us
    psum x1, waiting for transfers between devices, per_device(): lax.psum((grad_w_in, grad_b_in, grad_w_conv, grad_b_conv, grad_w_out, gra...  86 us
    psum x1, blocking collectives, per_device(): lax.psum((grad_w_in, grad_b_in, grad_w_conv, grad_b_conv, grad_w_out, gra...  66.6 us
    unnamed x133, local copies, waits for them, and re-layouts  57.8 us
    dot_general x9, matrix products, scores_of(): jnp.einsum('bqhd,bkhd->bhqk', queries, keys_all, preferred_element_type=j...  39.4 us
    convert_element_type x4, other arithmetic, attend_back(): grad_scores = (probs * (grad_probs - weighted)).astype(jnp.bfloat16)  31.7 us
    another operation x3, local copies, waits for them, and re-layouts, per_device(): jnp.stack([unpaired(mapped[1]), unpaired(mapped[2])])  31.5 us
  transfers between devices with their start and end apart: 14, of which 9 were waited for; matrix products, arithmetic and copies ran while one was open for 3% of the time, Pallas kernels for 0%

commit v1 on v0

v1 whole, which is shorter than its diff:
```python
import jax
import jax.numpy as jnp
from jax import lax
from jax.experimental import pallas as pl
from jax.experimental.pallas import tpu as pltpu
from jax.sharding import Mesh
from jax.sharding import PartitionSpec as P

ITEMS, ROWS, COLS, C, CIN, HEADS, HEAD, FF = 8, 4, 8, 320, 192, 8, 40, 1280
CELLS = ITEMS * ROWS * COLS
PART = ROWS * COLS
CHIPS = 64
HALF = CHIPS * PART
TEXT = 80
LANES = 128
WIDE = 256
SCALE = HEAD**-0.5
LOG2E = 1.4426950408889634
EPS = 1e-5
MASKED = -1e30
KEY, VALUE, MASK = HEAD, 2 * HEAD, 3 * HEAD
ACROSS = ("sp", "x")
SUM_ROWS = 4096

bf16, f32 = jnp.bfloat16, jnp.float32
NT = (((1,), (1,)), ((), ()))


def dot(left, right):
    return jnp.dot(left, right, preferred_element_type=f32)


def dot_nt(left, right):
    return lax.dot_general(left, right, NT, preferred_element_type=f32)


def lane_of(shape):
    return lax.broadcasted_iota(jnp.int32, shape, len(shape) - 1)


def moments(values):
    center = values - jnp.mean(values, -1, keepdims=True)
    rate = lax.rsqrt(jnp.mean(center * center, -1, keepdims=True) + EPS)
    return center * rate, rate


def norm_back(unit, rate, grads):
    return rate * (
        grads
        - jnp.mean(grads, -1, keepdims=True)
        - unit * jnp.mean(grads * unit, -1, keepdims=True)
    )


def call(kernel, outs, ins, name, scalars=0, scratch=(), vmem=48):
    return pl.pallas_call(
        kernel,
        out_shape=outs,
        in_specs=[
            pl.BlockSpec(memory_space=pltpu.SMEM if i < scalars else pltpu.VMEM)
            for i in range(len(ins))
        ],
        scratch_shapes=list(scratch),
        compiler_params=pltpu.CompilerParams(vmem_limit_bytes=vmem << 20),
        name=name,
    )(*ins)


def out(*shape, dtype=bf16):
    return jax.ShapeDtypeStruct(shape, dtype)


def adapter_kernel(
    place, valid, center, top, bottom, left, right, latent, w_in, w_conv, b_conv, w_out, b_out,
    w_qkv, rows_out, mixed_out, smooth_out, slope_out, cond_out,
):
    span = ITEMS * (ROWS + 2)
    block = jnp.concatenate(
        [top[...].astype(f32), center[...].astype(f32), bottom[...].astype(f32)], axis=1
    ).reshape(span, COLS, WIDE)
    col = lax.broadcasted_iota(jnp.int32, (span, COLS, WIDE), 1)
    near = jnp.where(
        col == 0, left[...].astype(f32).reshape(span, 1, WIDE), pltpu.roll(block, 1, 1)
    )
    far = jnp.where(
        col == COLS - 1,
        right[...].astype(f32).reshape(span, 1, WIDE),
        pltpu.roll(block, COLS - 1, 1),
    )
    inner = jnp.zeros((CELLS, C), f32)
    start_here = None
    for j, moved in enumerate((near, block, far)):
        start = dot(moved.reshape(span * COLS, WIDE).astype(bf16), w_in[...])
        start = start.reshape(ITEMS, ROWS + 2, COLS, C)
        moved = moved.reshape(ITEMS, ROWS + 2, COLS, WIDE)
        for i in range(3):
            patch = start[:, i : i + ROWS].reshape(CELLS, C).astype(bf16)
            if i == 1 and j == 1:
                start_here = patch.astype(f32)
            inner += dot(patch, w_conv[3 * i + j])
            cond_out[3 * i + j] = moved[:, i : i + ROWS].reshape(CELLS, WIDE).astype(bf16)
    inner += b_conv[...]
    gate = jax.nn.sigmoid(inner)
    smooth = (inner * gate).astype(bf16)
    smooth_out[...] = smooth
    slope_out[...] = gate * (1.0 + inner * (1.0 - gate))
    mixed = latent[...].astype(f32) + (start_here + dot(smooth, w_out[...]) + b_out[...])
    mixed_out[...] = mixed
    normed = moments(mixed)[0].astype(bf16)
    rows = dot(normed, w_qkv[...])
    lane = lane_of((PART, LANES))
    row = lax.broadcasted_iota(jnp.int32, (PART, LANES), 0) // COLS + ROWS * place[0]
    for item in range(ITEMS):
        hidden = jnp.where(row >= valid[item], MASKED, 0.0)
        extra = jnp.where(lane == MASK, hidden, jnp.where(lane > MASK, 1.0, 0.0))
        for head in range(HEADS):
            piece = rows[item * PART : (item + 1) * PART, head * LANES : (head + 1) * LANES]
            rows_out[item, head] = (piece + extra).astype(bf16)


def attend_kernel(own, other, packed_out, query_out, full_out, scores):
    block, step = scores.shape[0], 512
    chunks = [(ref, at) for ref in (own, other) for at in range(0, HALF, step)]

    def body(b, carry):
        rows = pl.ds(pl.multiple_of(b * block, block), block)
        lane = lane_of((block, LANES))
        query = pltpu.roll(own[rows, :].astype(f32), KEY, 1)
        query = jnp.where(
            (lane >= KEY) & (lane < VALUE), query, jnp.where(lane == MASK, 1.0, 0.0)
        )
        query_low = query.astype(bf16)
        peak = None
        for n, (ref, at) in enumerate(chunks):
            part = dot_nt(query_low, ref[at : at + step, :])
            scores[:, n * step : (n + 1) * step] = part
            for t in range(0, step, LANES):
                piece = part[:, t : t + LANES]
                peak = piece if peak is None else jnp.maximum(peak, piece)
        peak = jnp.max(peak, axis=1, keepdims=True)
        shift = peak * (SCALE * LOG2E)
        total = jnp.zeros((block, LANES), f32)
        for n, (ref, at) in enumerate(chunks):
            part = scores[:, n * step : (n + 1) * step]
            probs = jnp.exp2(part * (SCALE * LOG2E) - shift).astype(bf16)
            total += dot(probs, ref[at : at + step, :])
        mass = jnp.sum(jnp.where(lane == MASK + 1, total, 0.0), axis=1, keepdims=True)
        total = total / mass
        logsum = peak + jnp.log(mass) * (1.0 / SCALE)
        first = logsum.astype(bf16).astype(f32)
        second = (logsum - first).astype(bf16).astype(f32)
        third = logsum - first - second
        for n, piece in enumerate((first, second, third)):
            query = jnp.where(lane == MASK + 1 + n, -piece, query)
        query_out[rows, :] = query.astype(bf16)
        full_out[rows, :] = total
        pairs = total.reshape(block // PART, 2, PART // 2, LANES)
        lane = lane_of((block // 2, LANES))
        low = pltpu.roll(pairs[:, 0].reshape(block // 2, LANES), LANES - VALUE, 1)
        high = pltpu.roll(pairs[:, 1].reshape(block // 2, LANES), LANES - VALUE + HEAD, 1)
        packed = jnp.where(lane < HEAD, low, jnp.where(lane < 2 * HEAD, high, 0.0))
        packed = packed.astype(bf16).reshape(block // PART, PART // 2, LANES)
        packed_out[pl.ds(b * (block // PART), block // PART)] = packed
        return carry

    lax.fori_loop(0, HALF // block, body, 0)


def middle_kernel(
    lengths, heads_in, mixed, cotangent, text_keys, text_values, w_attn, b_attn, w_cross_query,
    w_cross_out, b_cross, w_ff_in, b_ff_in, w_ff_out, b_ff_out, result_out, grad_out, heads_out,
    probs_keep,
):
    half = CELLS // 2
    split = w_attn.shape[1] // 2
    packed = jnp.concatenate(
        [heads_in[:, head].reshape(half, LANES) for head in range(HEADS)], axis=1
    )
    both = dot(packed, w_attn[...])
    shape = (ITEMS, 1, PART // 2, C)
    attended = jnp.concatenate(
        [both[:, :C].reshape(shape), both[:, split : split + C].reshape(shape)], axis=1
    ).reshape(CELLS, C)
    first = mixed[...] + attended + b_attn[...]
    unit_two, rate_two = moments(first)
    cross_query = dot(unit_two.astype(bf16), w_cross_query[...]).astype(bf16)
    lane = lane_of((PART, C))
    in_head = [(lane >= HEAD * h) & (lane < HEAD * (h + 1)) for h in range(HEADS)]

    def spread(values):
        return jnp.concatenate(
            [jnp.where(mask, values, jnp.zeros_like(values)) for mask in in_head], axis=0
        )

    def gather(values):
        total = jnp.zeros((PART, C), f32)
        for h, mask in enumerate(in_head):
            total = jnp.where(mask, values[h * PART : (h + 1) * PART], total)
        return total

    token = lane_of((HEADS * PART, TEXT))
    outs = []
    for item in range(ITEMS):
        cells = slice(item * PART, (item + 1) * PART)
        scores = dot_nt(spread(cross_query[cells]), text_keys[item]) * SCALE
        scores = jnp.where(token < lengths[item], scores, MASKED)
        weights = jnp.exp(scores - jnp.max(scores, -1, keepdims=True))
        probs = weights / jnp.sum(weights, -1, keepdims=True)
        probs_keep[item] = probs
        outs.append(gather(dot(probs.astype(bf16), text_values[item])))
    cross = jnp.concatenate(outs, axis=0).astype(bf16)
    second = first + dot(cross, w_cross_out[...]) + b_cross[...]
    unit_three, rate_three = moments(second)
    normed_three = unit_three.astype(bf16)
    upstream = cotangent[...]
    result = second + b_ff_out[...]
    grad_normed = jnp.zeros((CELLS, C), f32)
    step = 256
    for at in range(0, FF, step):
        values, gates = slice(at, at + step), slice(FF + at, FF + at + step)
        value = dot(normed_three, w_ff_in[:, values]) + b_ff_in[:, values]
        gate = dot(normed_three, w_ff_in[:, gates]) + b_ff_in[:, gates]
        normal = 0.5 + 0.5 * lax.erf(gate * (0.5**0.5))
        density = jnp.exp(gate * gate * -0.5) * 0.3989422804014327
        gelu = gate * normal
        result += dot((value * gelu).astype(bf16), w_ff_out[values, :])
        grad_act = dot_nt(upstream, w_ff_out[values, :])
        grad_value = (grad_act * gelu).astype(bf16)
        grad_gate = (grad_act * value * (normal + gate * density)).astype(bf16)
        grad_normed += dot_nt(grad_value, w_ff_in[:, values])
        grad_normed += dot_nt(grad_gate, w_ff_in[:, gates])
    result_out[...] = result.astype(bf16)
    grad_second = upstream.astype(f32) + norm_back(unit_three, rate_three, grad_normed)
    grad_cross = dot_nt(grad_second.astype(bf16), w_cross_out[...]).astype(bf16)
    outs = []
    for item in range(ITEMS):
        cells = slice(item * PART, (item + 1) * PART)
        grad_probs = dot_nt(spread(grad_cross[cells]), text_values[item])
        probs = probs_keep[item]
        weighted = jnp.sum(probs * grad_probs, -1, keepdims=True)
        grad_scores = (probs * (grad_probs - weighted)).astype(bf16)
        outs.append(gather(dot(grad_scores, text_keys[item])))
    grad_query = (jnp.concatenate(outs, axis=0) * SCALE).astype(bf16)
    grad_first = grad_second + norm_back(
        unit_two, rate_two, dot_nt(grad_query, w_cross_query[...])
    )
    grad_out[...] = grad_first
    pairs = grad_first.reshape(ITEMS, 2, PART // 2, C)
    gap = jnp.zeros((half, split - C), f32)
    both = jnp.concatenate(
        [pairs[:, 0].reshape(half, C), gap, pairs[:, 1].reshape(half, C), gap], axis=1
    ).astype(bf16)
    packed = dot_nt(both, w_attn[...]).astype(bf16)
    for head in range(HEADS):
        piece = packed[:, head * LANES : (head + 1) * LANES]
        heads_out[:, head] = piece.reshape(ITEMS, PART // 2, LANES)


def attend_back_kernel(own, other, query, full, packed, own_out, other_out, grads, turned, sums):
    block, step = 512, 512
    half = HALF // 2
    lane = lane_of((half, LANES))
    value_lane = (lane >= VALUE) & (lane < MASK)
    pairs = packed[...].reshape(half, LANES).astype(f32)
    low = jnp.where(value_lane, pltpu.roll(pairs, VALUE, 1), 0.0)
    high = jnp.where(value_lane, pltpu.roll(pairs, VALUE - HEAD, 1), 0.0)
    shape = (CHIPS, 1, PART // 2, LANES)
    upstream = jnp.concatenate([low.reshape(shape), high.reshape(shape)], axis=1)
    upstream = upstream.reshape(HALF, LANES)
    lane = lane_of((HALF, LANES))
    weighted = jnp.sum(upstream * full[...], axis=1, keepdims=True)
    first = weighted.astype(bf16).astype(f32)
    upstream = jnp.where(lane == MASK + 4, -first, upstream)
    upstream = jnp.where(lane == MASK + 5, first - weighted, upstream)
    grads[...] = upstream.astype(bf16)
    turned[:, :HALF] = jnp.transpose(own[...])
    turned[:, HALF:] = jnp.transpose(other[...])
    sums[...] = jnp.zeros_like(sums)
    chunks = [(ref, at) for ref in (own, other) for at in range(0, HALF, step)]

    def body(b, carry):
        rows = pl.ds(pl.multiple_of(b * block, block), block)
        queries, upstream = query[rows, :], grads[rows, :]
        right = jnp.concatenate([queries, upstream], axis=0)
        grad_query = jnp.zeros((LANES, block), f32)
        for n, (ref, at) in enumerate(chunks):
            keys = ref[at : at + step, :]
            probs = jnp.exp2(dot_nt(keys, queries) * (SCALE * LOG2E))
            grad_scores = (probs * dot_nt(keys, upstream)).astype(bf16)
            both = jnp.concatenate([grad_scores, probs.astype(bf16)], axis=1)
            sums[n * step : (n + 1) * step, :] += dot(both, right)
            grad_query += dot(turned[:, n * step : (n + 1) * step], grad_scores)
        grad_query = jnp.transpose(grad_query) * SCALE
        own_out[rows, :] = pltpu.roll(grad_query, LANES - KEY, 1)
        return carry

    lax.fori_loop(0, HALF // block, body, 0)
    scale = jnp.where(lane < VALUE, SCALE, 1.0)
    rest = jnp.where(lane < MASK, sums[:HALF, :] * scale, 0.0)
    own_out[...] = jnp.where(lane < KEY, own_out[...], rest)
    rest = jnp.where((lane >= KEY) & (lane < MASK), sums[HALF:, :] * scale, 0.0)
    other_out[...] = rest.astype(bf16)


def finish_kernel(
    place, rows, w_qkv, mixed, grad_first, slope, smooth, cond, w_out, latent_out, parts_out
):
    joined = jnp.concatenate(
        [rows[:, head].reshape(CELLS, LANES) for head in range(HEADS)], axis=1
    )
    unit, rate = moments(mixed[...])
    latent = grad_first[...] + norm_back(unit, rate, dot_nt(joined, w_qkv[...]))
    latent_out[...] = latent
    branch = latent.astype(bf16)
    inner = (dot_nt(branch, w_out[...]) * slope[...]).astype(bf16)
    inner_turned = jnp.transpose(inner)
    branch_turned = jnp.transpose(branch)
    here, there = place[1], 1 - place[1]

    def put(side, at, values):
        values = values.astype(bf16)
        for t in range(0, values.shape[1], LANES):
            parts_out[side, at : at + C, :] = values[:, t : t + LANES]
            at += C
        return at

    at = 0
    for n in range(6):
        at = put(here, at, dot(inner_turned, cond[n]))
    parts_out[here, at:, :] = jnp.zeros((SUM_ROWS - at, LANES), bf16)
    at = 0
    for n in range(6, 9):
        at = put(there, at, dot(inner_turned, cond[n]))
    at = put(there, at, dot(branch_turned, cond[4]))
    last = jnp.concatenate([smooth[...], jnp.zeros((CELLS, 384 - C), bf16)], axis=1)
    at = put(there, at, dot(branch_turned, last))
    parts_out[there, at:, :] = jnp.zeros((SUM_ROWS - at, LANES), bf16)


def weights_kernel(
    place, mine, theirs, w_in, w_conv, win_out, bin_out, wconv_out, bconv_out, wout_out, bout_out,
    total,
):
    here = place[1]
    total[here] = mine[...]
    total[1 - here] = theirs[...]

    def take(side, at, count):
        return jnp.concatenate(
            [total[side, at + C * t : at + C * (t + 1), :] for t in range(count)], axis=1
        )

    grad_in = jnp.zeros((C, WIDE), f32)
    for n in range(9):
        moment = take(n // 6, 2 * C * (n % 6), 2)
        wconv_out[n] = dot_nt(w_in[...], moment)
        grad_in += dot(w_conv[n], moment)
        if n == 4:
            bconv_out[...] = jnp.transpose(moment.astype(f32))[CIN : CIN + 1, :]
    moment = jnp.transpose(take(1, 6 * C, 2).astype(f32))
    grad_in = jnp.transpose(grad_in) + moment
    win_out[...] = grad_in[:CIN]
    bin_out[...] = grad_in[CIN : CIN + 1]
    bout_out[...] = moment[CIN : CIN + 1]
    wout_out[...] = jnp.transpose(take(1, 8 * C, 3).astype(f32))[:C]


def swap(array):
    return lax.ppermute(array, "c", [(0, 1), (1, 0)])


def across(blocks):
    return lax.all_to_all(blocks, ACROSS, 0, 0, tiled=True)


def pieces(values, count):
    kept = []
    for _ in range(count):
        piece = values.astype(bf16)
        kept.append(piece)
        values = values - piece.astype(f32)
    return kept


def per_device(
    latent, condition, text_states, valid_rows, text_lengths, w_in, b_in, w_conv, b_conv, w_out,
    b_out, w_query, w_key, w_value, w_attn_out, b_attn_out, w_cross_query, w_cross_key,
    w_cross_value, w_cross_out, b_cross_out, w_ff_in, b_ff_in, w_ff_out, b_ff_out, cotangent,
):
    place = jnp.stack([lax.axis_index("sp"), lax.axis_index("c")]).astype(jnp.int32)

    ones = jnp.ones(condition.shape[:3] + (3,), bf16)
    center = jnp.pad(
        jnp.concatenate([condition, ones], axis=-1), ((0, 0),) * 3 + ((0, WIDE - CIN - 3),)
    )
    down = [(i, i + 1) for i in range(15)]
    top = lax.ppermute(center[:, ROWS - 1 :], "sp", down)
    bottom = lax.ppermute(center[:, :1], "sp", [(b, a) for a, b in down])
    tall = jnp.concatenate([top, center, bottom], axis=1)
    right_way = [(i, i + 1) for i in range(7)]
    span = ITEMS * (ROWS + 2)
    left = lax.ppermute(tall[:, :, COLS - 1].reshape(span, WIDE), ("x", "c"), right_way)
    right = lax.ppermute(
        tall[:, :, 0].reshape(span, WIDE), ("x", "c"), [(b, a) for a, b in right_way]
    )

    w_in_wide = jnp.concatenate(
        [w_in] + [piece[None] for piece in pieces(b_in, 3)], axis=0
    )
    w_in_wide = jnp.pad(w_in_wide, ((0, WIDE - CIN - 3), (0, 0)))
    w_qkv = jnp.concatenate(
        [w.reshape(C, HEADS, HEAD) for w in (w_query, w_key, w_value)], axis=-1
    )
    w_qkv = jnp.pad(w_qkv, ((0, 0), (0, 0), (0, LANES - 3 * HEAD))).reshape(C, HEADS * LANES)
    by_head = w_attn_out.reshape(HEADS, HEAD, C)
    w_attn = jnp.concatenate(
        [
            jnp.pad(by_head, ((0, 0), (at, LANES - HEAD - at), (0, 384 - C)))
            for at in (0, HEAD)
        ],
        axis=-1,
    ).reshape(HEADS * LANES, 768)
    text = jnp.pad(text_states, ((0, 0), (0, TEXT - text_states.shape[1]), (0, 0)))
    text_keys = jnp.einsum("btc,cd->btd", text, w_cross_key, preferred_element_type=f32)
    text_values = jnp.einsum("btc,cd->btd", text, w_cross_value, preferred_element_type=f32)
    text_keys, text_values = text_keys.astype(bf16), text_values.astype(bf16)
    taps = w_conv.reshape(9, C, C)

    rows, mixed, smooth, slope, cond = call(
        adapter_kernel,
        (
            out(ITEMS, HEADS, PART, LANES),
            out(CELLS, C, dtype=f32),
            out(CELLS, C),
            out(CELLS, C, dtype=f32),
            out(9, CELLS, WIDE),
        ),
        (
            place, valid_rows, center, top, bottom, left, right, latent.reshape(CELLS, C),
            w_in_wide, taps, b_conv[None], w_out, b_out[None], w_qkv,
        ),
        "adapter",
        scalars=2,
    )

    own = across(rows.reshape(CHIPS, PART, LANES)).reshape(HALF, LANES)
    other = swap(own)
    packed, query, full = call(
        attend_kernel,
        (out(CHIPS, PART // 2, LANES), out(HALF, LANES), out(HALF, LANES, dtype=f32)),
        (own, other),
        "attend",
        scratch=[pltpu.VMEM((256, 2 * HALF), f32)],
    )
    heads_in = across(packed).reshape(ITEMS, HEADS, PART // 2, LANES)

    result, grad_first, heads_out = call(
        middle_kernel,
        (out(CELLS, C), out(CELLS, C, dtype=f32), out(ITEMS, HEADS, PART // 2, LANES)),
        (
            text_lengths, heads_in, mixed, cotangent.reshape(CELLS, C), text_keys, text_values,
            w_attn, b_attn_out[None], w_cross_query, w_cross_out, b_cross_out[None], w_ff_in,
            b_ff_in[None], w_ff_out, b_ff_out[None],
        ),
        "middle",
        scalars=1,
        scratch=[pltpu.VMEM((ITEMS, HEADS * PART, TEXT), f32)],
    )

    grads_in = across(heads_out.reshape(CHIPS, PART // 2, LANES))
    own_grads, other_grads = call(
        attend_back_kernel,
        (out(HALF, LANES, dtype=f32), out(HALF, LANES)),
        (own, other, query, full, grads_in),
        "attend_back",
        scratch=[
            pltpu.VMEM((HALF, LANES), bf16),
            pltpu.VMEM((LANES, 2 * HALF), bf16),
            pltpu.VMEM((2 * HALF, LANES), f32),
        ],
    )
    row_grads = (own_grads + swap(other_grads).astype(f32)).astype(bf16)
    row_grads = across(row_grads.reshape(CHIPS, PART, LANES))

    latent_grad, parts = call(
        finish_kernel,
        (out(CELLS, C, dtype=f32), out(2, SUM_ROWS, LANES)),
        (
            place, row_grads.reshape(ITEMS, HEADS, PART, LANES), w_qkv, mixed, grad_first, slope,
            smooth, cond, w_out,
        ),
        "finish",
        scalars=1,
    )

    shares = (parts[0].astype(f32) + swap(parts[1]).astype(f32)).astype(bf16)
    shares = across(shares.reshape(CHIPS, SUM_ROWS // CHIPS, LANES))
    share = jnp.sum(shares.astype(f32), axis=0).astype(bf16)
    mine = across(jnp.broadcast_to(share[None], shares.shape)).reshape(SUM_ROWS, LANES)
    theirs = swap(mine)
    grad_w_in, grad_b_in, grad_w_conv, grad_b_conv, grad_w_out, grad_b_out = call(
        weights_kernel,
        (
            out(CIN, C, dtype=f32),
            out(1, C, dtype=f32),
            out(9, C, C, dtype=f32),
            out(1, C, dtype=f32),
            out(C, C, dtype=f32),
            out(1, C, dtype=f32),
        ),
        (place, mine, theirs, w_in_wide.T, taps),
        "weights",
        scalars=1,
        scratch=[pltpu.VMEM((2, SUM_ROWS, LANES), bf16)],
    )
    grid = (ITEMS, ROWS, COLS, C)
    return (
        result.reshape(grid),
        latent_grad.reshape(grid),
        grad_w_in,
        grad_b_in[0],
        grad_w_conv.reshape(3, 3, C, C),
        grad_b_conv[0],
        grad_w_out,
        grad_b_out[0],
    )


def solution(mesh):
    split = Mesh(mesh.devices.reshape(16, 4, 2), ("sp", "x", "c"))
    cells = P(None, "sp", ("x", "c"), None)
    in_specs = (cells, cells) + (P(),) * 23 + (cells,)
    out_specs = (cells, cells) + (P(),) * 6
    return jax.shard_map(
        per_device, mesh=split, in_specs=in_specs, out_specs=out_specs, check_vma=False
    )
```

time: 817 us -> 234 us (0.29)
  waiting for transfers between devices: 299 us -> 12.4 us
  local copies, waits for them, and re-layouts: 185 us -> 17 us
  matrix products: 127 us -> 4.3 us
  Pallas kernels: 0 us -> 65.8 us
  other arithmetic: 61.1 us -> 6.01 us
  blocking collectives: 81.6 us -> 102 us
  starting transfers between devices: 38.9 us -> 24.3 us
  between operations: 15.2 us -> 1.29 us
    dot_general x58 -> x2, matrix products: 127 us -> 4.3 us  [the longest x1 2.8 us: per_device(): jnp.einsum('btc,cd->btd', text, w_cross_key, preferred_element_type=f32)]
    all_gather x1 -> x0, waiting for transfers between devices: 107 us -> none  [per_device(): gathered = lax.all_gather(own_pair, 'sp', axis=2, tiled=True)]
    reduce_scatter x1 -> x0, waiting for transfers between devices: 87.3 us -> none  [per_device(): lax.psum_scatter(partial_kv.astype(jnp.bfloat16), 'sp', scatter_dimension...]
    all_to_all x1 -> x5, blocking collectives: 14.9 us -> 102 us  [across(): return lax.all_to_all(blocks, ACROSS, 0, 0, tiled=True)]
    psum x1 -> x0, waiting for transfers between devices: 86 us -> none  [per_device(): lax.psum((grad_w_in, grad_b_in, grad_w_conv, grad_b_conv, grad_w_out, gra...]
    psum x1 -> x0, blocking collectives: 66.6 us -> none  [per_device(): lax.psum((grad_w_in, grad_b_in, grad_w_conv, grad_b_conv, grad_w_out, gra...]
    pallas_call x0 -> x6, Pallas kernels: none -> 65.8 us  [call(): pl.pallas_call(kernel, out_shape=outs, in_specs=[pl.BlockSpec(memory_spac...]
    another operation x11 -> x2, local copies, waits for them, and re-layouts: 43.4 us -> 0.03 us  [the longest x1 0.01 us: per_device(): tall[:, :, 0].reshape(span, WIDE)]
  transfers between devices with their start and end apart: 14 -> 9, of which waited for: 9 -> 5; matrix products, arithmetic and copies ran while one was open for 3% -> 6% of each run, Pallas kernels for 0% -> 0%
where the time goes in v1:
time: 234 us; the launch traced here: 233 us
  blocking collectives  102 us (44%)
  Pallas kernels  65.8 us (28%)
  starting transfers between devices  24.3 us (10%)
  local copies, waits for them, and re-layouts  17 us (7%)
  waiting for transfers between devices  12.4 us (5%)
  other arithmetic  6.01 us (3%)
  matrix products  4.3 us (2%)
    all_to_all x5, blocking collectives, across(): return lax.all_to_all(blocks, ACROSS, 0, 0, tiled=True)  102 us
    pallas_call x6, Pallas kernels, call(): pl.pallas_call(kernel, out_shape=outs, in_specs=[pl.BlockSpec(memory_spac...  65.8 us
    unnamed x96, local copies, waits for them, and re-layouts  15.8 us
    ppermute x4, starting transfers between devices, swap(): return lax.ppermute(array, 'c', [(0, 1), (1, 0)])  7.27 us
    ppermute x4, waiting for transfers between devices, swap(): return lax.ppermute(array, 'c', [(0, 1), (1, 0)])  5.95 us
    all_to_all x1, starting transfers between devices, across(): return lax.all_to_all(blocks, ACROSS, 0, 0, tiled=True)  4.81 us
  transfers between devices with their start and end apart: 9, of which 5 were waited for; matrix products, arithmetic and copies ran while one was open for 6% of the time, Pallas kernels for 0%

profile of v1, /device:TPU:1, one launch (start us, length us, event | category | flops | bytes accessed | tf_op | source)
XLA Modules:
  0.0 233.1 jit_solution(9982312773329963845)
XLA Ops:
  3.0 4.7 %collective-permute-start = (bf16[8,1,8,256]{3,2,1,0:T(8,128)(2,1)S(1)}, bf16[8,1,8,256]{3,2,1,0:T(8,128)(2,1)S(1)}, u32[]{:S(2)}, u32[]{:S(2)}) collective-permute-start(bf16[8,1,8,256]{3,2,1,0:T(8,128)(2,1)S(1)} %get-tuple-element.53), channel_id=1, source_target_pairs={{0,8},{8,16},{16,24},{24,32},{32,40},{40,48},{48,56},{56,64},{64,7... | collective-permute-start | bytes 98312 | tf_op jit(solution)/shard_map/ppermute | solution.py:397
  13.1 4.4 %collective-permute-start.2 = (bf16[48,256]{1,0:T(8,128)(2,1)S(1)}, bf16[48,256]{1,0:T(8,128)(2,1)S(1)}, u32[]{:S(2)}, u32[]{:S(2)}) collective-permute-start(bf16[48,256]{1,0:T(8,128)(2,1)S(1)} %reshape_squeeze.6), channel_id=1, source_target_pairs={{0,1},{1,2},{2,3},{3,4},{4,5},{5,6},{6,7},{8,9},{9,10},{10,11},{11... | collective-permute-start | bytes 73736 | tf_op jit(solution)/shard_map/ppermute | solution.py:402
  17.5 1.9 collective-permute-start.3
  20.0 2.7 %collective-permute-done.3.right = bf16[48,256]{1,0:T(8,128)(2,1)S(1)} collective-permute-done((bf16[48,256]{1,0:T(8,128)(2,1)S(1)}, bf16[48,256]{1,0:T(8,128)(2,1)S(1)}, u32[]{:S(2)}, u32[]{:S(2)}) %collective-permute-start.3) | collective-permute-done | bytes 24608 | tf_op jit(solution)/shard_map/ppermute | solution.py:403
  22.7 4.4 %adapter.1 = (bf16[8,8,32,128]{3,2,1,0:T(8,128)(2,1)S(1)}, f32[256,320]{1,0:T(8,128)S(1)}, bf16[256,320]{1,0:T(8,128)(2,1)S(1)}, f32[256,320]{1,0:T(8,128)S(1)}, bf16[9,256,256]{2,1,0:T(8,128)(2,1)S(1)}) custom-call(s32[2]{0:T(128)S(1)} %pad_add_fusion.place, s32[8]{0:T(128)S(1)} %copy-done.26, bf16[8,4,8,256]{3,2,1,0:T(8,128)(2,1)S(1)} %fusion.17.center, ...), custom_call_target="tpu_custom_call" | custom-call | tf_op jit(solution)/shard_map/adapter/pallas_call | solution.py:56
  27.1 26.1 %all_to_all.30 = bf16[64,32,128]{2,1,0:T(8,128)(2,1)S(1)} all-to-all(bf16[64,32,128]{2,1,0:T(8,128)(2,1)S(1)} %bitcast.45), channel_id=1, replica_groups=mesh['sp'=16,'x'=4,'c'=2] {'sp','x'}, dimensions={0} | all-to-all | bytes 1048576 | tf_op jit(solution)/shard_map/all_to_all | solution.py:373
  55.4 19.0 %attend.1 = (bf16[64,16,128]{2,1,0:T(8,128)(2,1)}, bf16[2048,128]{1,0:T(8,128)(2,1)S(1)}, f32[2048,128]{1,0:T(8,128)S(1)}) custom-call(bf16[2048,128]{1,0:T(8,128)(2,1)S(1)} %bitcast.39, bf16[2048,128]{1,0:T(8,128)(2,1)S(1)} %collective-permute-done.4.other), custom_call_target="tpu_custom_call" | custom-call | tf_op jit(solution)/shard_map/attend/pallas_call | solution.py:56
  76.9 4.8 %all-to-all-start.1 = ((bf16[64,16,128]{2,1,0:T(8,128)(2,1)}), bf16[64,16,128]{2,1,0:T(8,128)(2,1)S(1)}, u32[]{:S(2)}, u32[]{:S(2)}) async-start(bf16[64,16,128]{2,1,0:T(8,128)(2,1)} %get-tuple-element.30), calls=%async_computation.1 | async-start | bytes 524288 | tf_op jit(solution)/shard_map/all_to_all | solution.py:373
  83.1 2.2 copy.48.w_ff_out
  85.3 2.8 %convolution_convert_fusion.1.text_keys = bf16[8,80,320]{2,1,0:T(8,128)(2,1)} fusion(bf16[8,77,768]{2,1,0:T(8,128)(2,1)} %copy-done.30, bf16[768,320]{0,1:T(8,128)(2,1)} %param.43), kind=kOutput, calls=%fused_computation.12 | convolution fusion | flops 314777600 | bytes 1847296 | tf_op jit(solution)/shard_map/btc,cd->btd/dot_general | solution.py:424
  88.1 3.8 %all-to-all-done.1 = bf16[64,16,128]{2,1,0:T(8,128)(2,1)S(1)} async-done(((bf16[64,16,128]{2,1,0:T(8,128)(2,1)}), bf16[64,16,128]{2,1,0:T(8,128)(2,1)S(1)}, u32[]{:S(2)}, u32[]{:S(2)}) %all-to-all-start.1) | async-done | bytes 262176 | tf_op jit(solution)/shard_map/all_to_all | solution.py:373
  98.9 13.1 %middle.1 = (bf16[256,320]{1,0:T(8,128)(2,1)}, f32[256,320]{1,0:T(8,128)S(1)}, bf16[8,8,16,128]{3,2,1,0:T(8,128)(2,1)S(1)}) custom-call(s32[8]{0:T(128)S(1)} %copy-done.27, bf16[8,8,16,128]{3,2,1,0:T(8,128)(2,1)S(1)} %bitcast.44, f32[256,320]{1,0:T(8,128)S(1)} %copy-done.6, bf16[256,320]{1,0:T(8,128)(2,1)S(1)} %bitcast.48, ...), custom_call_target="tpu_custom_call" | custom-call | tf_op jit(solution)/shard_map/middle/pallas_call | solution.py:56
  112.0 15.5 %all_to_all.31.packed = bf16[64,16,128]{2,1,0:T(8,128)(2,1)S(1)} all-to-all(bf16[64,16,128]{2,1,0:T(8,128)(2,1)S(1)} %bitcast.46), channel_id=1, replica_groups=mesh['sp'=16,'x'=4,'c'=2] {'sp','x'}, dimensions={0} | all-to-all | bytes 524288 | tf_op jit(solution)/shard_map/all_to_all | solution.py:373
  127.6 22.3 %attend_back.1 = (f32[2048,128]{1,0:T(8,128)S(1)}, bf16[2048,128]{1,0:T(8,128)(2,1)S(1)}) custom-call(bf16[2048,128]{1,0:T(8,128)(2,1)S(1)} %bitcast.40, bf16[2048,128]{1,0:T(8,128)(2,1)S(1)} %copy-done.4, bf16[2048,128]{1,0:T(8,128)(2,1)S(1)} %copy-done.15, f32[2048,128]{1,0:T(8,128)S(1)} %copy-done.11, bf16[64,16,128]{2,1,0:T(8,128)(2,1)S(1)} %all_to_all.31.packed), custom_call_target="tpu_custom_call" | custom-call | tf_op jit(solution)/shard_map/attend_back/pallas_call | solution.py:56
  149.9 1.7 collective-permute-start.5
  153.3 16.8 %all_to_all.32 = bf16[64,32,128]{2,1,0:T(8,128)(2,1)S(1)} all-to-all(bf16[64,32,128]{2,1,0:T(8,128)(2,1)S(1)} %bitcast.51), channel_id=1, replica_groups=mesh['sp'=16,'x'=4,'c'=2] {'sp','x'}, dimensions={0} | all-to-all | bytes 1048576 | tf_op jit(solution)/shard_map/all_to_all | solution.py:373
  170.1 2.5 %finish.1 = (f32[256,320]{1,0:T(8,128)}, bf16[2,4096,128]{2,1,0:T(8,128)(2,1)S(1)}) custom-call(s32[2]{0:T(128)S(1)} %pad_add_fusion.place, bf16[8,8,32,128]{3,2,1,0:T(8,128)(2,1)S(1)} %bitcast.43, bf16[320,1024]{1,0:T(8,128)(2,1)S(1)} %copy.49.w_qkv, f32[256,320]{1,0:T(8,128)S(1)} %copy-done.7, f32[256,320]{1,0:T(8,128)S(1)} %get-tuple-element.38.grad_first, ...), custom_call_target="tpu_custom_call" | custom-call | tf_op jit(solution)/shard_map/finish/pallas_call | solution.py:56
  172.7 2.0 collective-permute-start.6
  174.7 2.3 collective-permute-done.6
  177.2 22.3 %all_to_all.33 = bf16[64,64,128]{2,1,0:T(8,128)(2,1)S(1)} all-to-all(bf16[64,64,128]{2,1,0:T(8,128)(2,1)S(1)} %bitcast.49), channel_id=1, replica_groups=mesh['sp'=16,'x'=4,'c'=2] {'sp','x'}, dimensions={0} | all-to-all | bytes 2097152 | tf_op jit(solution)/shard_map/all_to_all | solution.py:373
  200.0 21.1 %all_to_all.34 = bf16[64,64,128]{2,1,0:T(8,128)(2,1)S(1)} all-to-all(bf16[64,64,128]{2,1,0:T(8,128)(2,1)S(1)} %broadcast_in_dim.43), channel_id=1, replica_groups=mesh['sp'=16,'x'=4,'c'=2] {'sp','x'}, dimensions={0} | all-to-all | bytes 2097152 | tf_op jit(solution)/shard_map/all_to_all | solution.py:373
  221.2 3.2 %collective-permute-start.7 = (bf16[4096,128]{1,0:T(8,128)(2,1)S(1)}, bf16[4096,128]{1,0:T(8,128)(2,1)S(1)}, u32[]{:S(2)}, u32[]{:S(2)}) collective-permute-start(bf16[4096,128]{1,0:T(8,128)(2,1)S(1)} %bitcast.41), channel_id=1, source_target_pairs={{0,1},{1,0},{2,3},{3,2},{4,5},{5,4},{6,7},{7,6},{8,9},{9,8},{10,11... | collective-permute-start | bytes 3145736 | tf_op jit(solution)/shard_map/ppermute | solution.py:369
  224.5 2.1 collective-permute-done.7.theirs
  226.6 4.6 %weights.1 = (f32[192,320]{1,0:T(8,128)}, f32[1,320]{1,0:T(1,128)S(1)}, f32[9,320,320]{2,1,0:T(8,128)}, f32[1,320]{1,0:T(1,128)S(1)}, f32[320,320]{1,0:T(8,128)}, /*index=5*/f32[1,320]{1,0:T(1,128)S(1)}) custom-call(s32[2]{0:T(128)S(1)} %pad_add_fusion.place, bf16[4096,128]{1,0:T(8,128)(2,1)S(1)} %bitcast.42, ...), custom_call_target="tpu_custom_call" | custom-call | tf_op jit(solution)/shard_map/weights/pallas_call | solution.py:56
  (133 shorter events, 25.5 us)
Async XLA Ops:
  0.6 53.1 %copy-start = (bf16[768,320]{0,1:T(8,128)(2,1)S(1)}, bf16[768,320]{0,1:T(8,128)(2,1)}, u32[]{:S(2)}) copy-start(bf16[768,320]{0,1:T(8,128)(2,1)} %param.44) | copy-start | bytes 1474564
  1.7 11.1 %collective-permute-start.1 = (bf16[8,1,8,256]{3,2,1,0:T(8,128)(2,1)S(1)}, bf16[8,1,8,256]{3,2,1,0:T(8,128)(2,1)S(1)}, u32[]{:S(2)}, u32[]{:S(2)}) collective-permute-start(bf16[8,1,8,256]{3,2,1,0:T(8,128)(2,1)S(1)} %get-tuple-element.52), channel_id=1, source_target_pairs={{8,0},{16,8},{24,16},{32,24},{40,32},{48,40},{56,48},{64,56},{72,6... | collective-permute-start | bytes 98312 | tf_op jit(solution)/shard_map/ppermute | solution.py:398
  3.0 9.8 %collective-permute-start = (bf16[8,1,8,256]{3,2,1,0:T(8,128)(2,1)S(1)}, bf16[8,1,8,256]{3,2,1,0:T(8,128)(2,1)S(1)}, u32[]{:S(2)}, u32[]{:S(2)}) collective-permute-start(bf16[8,1,8,256]{3,2,1,0:T(8,128)(2,1)S(1)} %get-tuple-element.53), channel_id=1, source_target_pairs={{0,8},{8,16},{16,24},{24,32},{32,40},{40,48},{48,56},{56,64},{64,7... | collective-permute-start | bytes 98312 | tf_op jit(solution)/shard_map/ppermute | solution.py:397
  13.1 6.9 %collective-permute-start.2 = (bf16[48,256]{1,0:T(8,128)(2,1)S(1)}, bf16[48,256]{1,0:T(8,128)(2,1)S(1)}, u32[]{:S(2)}, u32[]{:S(2)}) collective-permute-start(bf16[48,256]{1,0:T(8,128)(2,1)S(1)} %reshape_squeeze.6), channel_id=1, source_target_pairs={{0,1},{1,2},{2,3},{3,4},{4,5},{5,6},{6,7},{8,9},{9,10},{10,11},{11... | collective-permute-start | bytes 73736 | tf_op jit(solution)/shard_map/ppermute | solution.py:402
  17.5 5.1 %collective-permute-start.3 = (bf16[48,256]{1,0:T(8,128)(2,1)S(1)}, bf16[48,256]{1,0:T(8,128)(2,1)S(1)}, u32[]{:S(2)}, u32[]{:S(2)}) collective-permute-start(bf16[48,256]{1,0:T(8,128)(2,1)S(1)} %reshape_squeeze.7), channel_id=1, source_target_pairs={{1,0},{2,1},{3,2},{4,3},{5,4},{6,5},{7,6},{9,8},{10,9},{11,10},{12... | collective-permute-start | bytes 73736 | tf_op jit(solution)/shard_map/ppermute | solution.py:403
  22.6 31.0 %copy-start.31 = (bf16[8,77,768]{2,0,1:T(8,128)(2,1)S(1)}, bf16[8,77,768]{2,0,1:T(8,128)(2,1)}, u32[]{:S(2)}) copy-start(bf16[8,77,768]{2,0,1:T(8,128)(2,1)} %param.28) | copy-start | bytes 2838532
  27.0 28.3 %copy-start.5 = (f32[256,320]{1,0:T(8,128)}, f32[256,320]{1,0:T(8,128)S(1)}, u32[]{:S(2)}) copy-start(f32[256,320]{1,0:T(8,128)S(1)} %get-tuple-element.31.mixed) | copy-start | bytes 983044
  27.0 28.3 %copy-start.8 = (bf16[9,256,256]{2,1,0:T(8,128)(2,1)}, bf16[9,256,256]{2,1,0:T(8,128)(2,1)S(1)}, u32[]{:S(2)}) copy-start(bf16[9,256,256]{2,1,0:T(8,128)(2,1)S(1)} %get-tuple-element.41.cond) | copy-start | bytes 3538948
  27.0 28.3 %copy-start.18 = (f32[256,320]{1,0:T(8,128)}, f32[256,320]{1,0:T(8,128)S(1)}, u32[]{:S(2)}) copy-start(f32[256,320]{1,0:T(8,128)S(1)} %get-tuple-element.39.slope) | copy-start | bytes 983044
  27.1 28.3 %copy-start.24 = (bf16[256,320]{1,0:T(8,128)(2,1)}, bf16[256,320]{1,0:T(8,128)(2,1)S(1)}, u32[]{:S(2)}) copy-start(bf16[256,320]{1,0:T(8,128)(2,1)S(1)} %get-tuple-element.40.smooth) | copy-start | bytes 491524
  53.2 2.2 collective-permute-start.4
  55.3 27.6 %copy-start.42 = (f32[320]{0:T(512)S(1)}, f32[320]{0:T(512)}, u32[]{:S(2)}) copy-start(f32[320]{0:T(512)} %param.41) | copy-start | bytes 3844
  55.3 27.6 %copy-start.43 = (f32[320]{0:T(512)S(1)}, f32[320]{0:T(512)}, u32[]{:S(2)}) copy-start(f32[320]{0:T(512)} %param.46) | copy-start | bytes 3844
  55.3 27.7 %copy-start.44 = (f32[320]{0:T(512)S(1)}, f32[320]{0:T(512)}, u32[]{:S(2)}) copy-start(f32[320]{0:T(512)} %param.50) | copy-start | bytes 3844
  55.4 27.7 %copy-start.39 = (f32[2560]{0:T(1024)S(1)}, f32[2560]{0:T(1024)}, u32[]{:S(2)}) copy-start(f32[2560]{0:T(1024)} %param.48) | copy-start | bytes 30724
  76.9 14.9 %all-to-all-start.1 = ((bf16[64,16,128]{2,1,0:T(8,128)(2,1)}), bf16[64,16,128]{2,1,0:T(8,128)(2,1)S(1)}, u32[]{:S(2)}, u32[]{:S(2)}) async-start(bf16[64,16,128]{2,1,0:T(8,128)(2,1)} %get-tuple-element.30), calls=%async_computation.1 | async-start | bytes 524288 | tf_op jit(solution)/shard_map/all_to_all | solution.py:373
  98.9 28.6 %copy-start.4 = (bf16[2048,128]{1,0:T(8,128)(2,1)S(1)}, bf16[2048,128]{1,0:T(8,128)(2,1)}, u32[]{:S(2)}) copy-start(bf16[2048,128]{1,0:T(8,128)(2,1)} %copy-done.3) | copy-start | bytes 1572868
  98.9 28.6 %copy-start.11 = (f32[2048,128]{1,0:T(8,128)S(1)}, f32[2048,128]{1,0:T(8,128)}, u32[]{:S(2)}) copy-start(f32[2048,128]{1,0:T(8,128)} %copy-done.10) | copy-start | bytes 3145732
  98.9 28.6 %copy-start.15 = (bf16[2048,128]{1,0:T(8,128)(2,1)S(1)}, bf16[2048,128]{1,0:T(8,128)(2,1)}, u32[]{:S(2)}) copy-start(bf16[2048,128]{1,0:T(8,128)(2,1)} %copy-done.14) | copy-start | bytes 1572868
  149.9 3.3 %collective-permute-start.5 = (bf16[2048,128]{1,0:T(8,128)(2,1)S(1)}, bf16[2048,128]{1,0:T(8,128)(2,1)S(1)}, u32[]{:S(2)}, u32[]{:S(2)}) collective-permute-start(bf16[2048,128]{1,0:T(8,128)(2,1)S(1)} %get-tuple-element.37), channel_id=1, source_target_pairs={{0,1},{1,0},{2,3},{3,2},{4,5},{5,4},{6,7},{7,6},{8,9},{9,8},{10,11... | collective-permute-start | bytes 1572872 | tf_op jit(solution)/shard_map/ppermute | solution.py:369
  172.7 4.3 %collective-permute-start.6 = (bf16[4096,128]{1,0:T(8,128)(2,1)S(1)}, bf16[4096,128]{1,0:T(8,128)(2,1)S(1)}, u32[]{:S(2)}, u32[]{:S(2)}) collective-permute-start(bf16[4096,128]{1,0:T(8,128)(2,1)S(1)} %slice_bitcast_fusion), channel_id=1, source_target_pairs={{0,1},{1,0},{2,3},{3,2},{4,5},{5,4},{6,7},{7,6},{8,9},{9,8},{10,11... | collective-permute-start | bytes 3145736 | tf_op jit(solution)/shard_map/ppermute | solution.py:369
  199.7 24.6 %copy-start.29 = (bf16[192,320]{0,1:T(8,128)(2,1)S(1)}, bf16[192,320]{0,1:T(8,128)(2,1)}, u32[]{:S(2)}) copy-start(bf16[192,320]{0,1:T(8,128)(2,1)} %copy-done.28) | copy-start | bytes 368644
  199.8 26.9 %copy-start.1 = (bf16[3,3,320,320]{3,2,1,0:T(8,128)(2,1)S(1)}, bf16[3,3,320,320]{3,2,1,0:T(8,128)(2,1)}, u32[]{:S(2)}) copy-start(bf16[3,3,320,320]{3,2,1,0:T(8,128)(2,1)} %param.33) | copy-start | bytes 5529604
  221.2 5.5 %collective-permute-start.7 = (bf16[4096,128]{1,0:T(8,128)(2,1)S(1)}, bf16[4096,128]{1,0:T(8,128)(2,1)S(1)}, u32[]{:S(2)}, u32[]{:S(2)}) collective-permute-start(bf16[4096,128]{1,0:T(8,128)(2,1)S(1)} %bitcast.41), channel_id=1, source_target_pairs={{0,1},{1,0},{2,3},{3,2},{4,5},{5,4},{6,7},{7,6},{8,9},{9,8},{10,11... | collective-permute-start | bytes 3145736 | tf_op jit(solution)/shard_map/ppermute | solution.py:369
  (30 other events, 268.0 us)
